TPU v7x, 256 devices: a whole 4x4x8 slice. The times are simulated.
256 devices in a mesh: dom: 32 (over z, y_lo, core), tile: 8 (over y_hi, x).
Axes of the slice: x: 4, y: 4 (y_hi: 2, y_lo: 2; y = y_hi * 2 + y_lo), z: 8, core: 2. Of those that a mesh axis runs over, the one named last changes fastest.
Arguments:
- state: float32 [64, 3, 256, 1024], P('dom', None, 'tile'), may hold values from -6 to 6
- noise: float32 [64, 256, 1024], P('dom', 'tile'), may hold values from -4 to 4
- parents: int32 [64], replicated, may hold values from 0 to 63, as said below
- measured_cell_position: int32 [16384], P('tile'), may hold values from 0 to 262143, as said below
- obs_value: float32 [16384], P('tile'), may hold values from -6 to 6
- obs_precision: float32 [16384], P('tile'), may hold values from 0.3 to 27
Outputs:
- predicted_fields: float32 [64, 3, 256, 1024], P('dom', None, 'tile')
- observation_mismatch: float32 [64], P('dom')
Inputs may be any that keep to these rules, and one draw needn't show every extreme that they name: parents never fall from one new particle to the next; the first is 0 and the last is 63. `measured_cell_position`: entries b * 2048 to (b + 1) * 2048 - 1 lie in rows b * 32 to (b + 1) * 32 - 1, all distinct; the first and last cell of those rows are observed.
All inputs are finite; a program needn't handle non-finite values.
Results may differ from a plain program's by a relative error of at most 0.00002.
Values sent between devices are 32-bit elements; how exact they have to be, the bound alone decides.
A program may use at most 128 MiB of HBM per device.

v0:
```python
import functools

import jax
import jax.numpy as jnp
from jax import lax
from jax.experimental import pallas as pl
from jax.experimental.pallas import tpu as pltpu
from jax.sharding import PartitionSpec as P

STEPS = 4
LANES = 128
HALO = 8
TALL = 48

COURANT = 1.2
CORIOLIS = 0.1
RELAXATION = 0.3

NOISE, GAIN, FIRST, SECOND = range(4)


def split_three(x):
    high = x.astype(jnp.bfloat16)
    rest = x - high.astype(jnp.float32)
    middle = rest.astype(jnp.bfloat16)
    low = (rest - middle.astype(jnp.float32)).astype(jnp.bfloat16)
    return high, middle, low


def kernel(
    n, tiles, cols, obs, obs_all,
    parents_in, position_in, value_in, precision_in, state, noise,
    result, mismatch_out,
    parents, position, value, precision,
    every0, every1, every2, pick0, pick1, pick2, fields, noise_all, nudge, weight, row_values, work, sums,
    spread_send, spread_recv, local_sem, back_send, back_recv, halo_send, halo_recv, sums_send, sums_recv,
):
    every = (every0, every1, every2)
    pick = (pick0, pick1, pick2)
    groups = cols // LANES
    dom = lax.axis_index("dom")
    tile = lax.axis_index("tile")
    has_above = tile > 0
    has_below = tile < tiles - 1

    def place(stage, j):
        column = pl.multiple_of((j % groups) * LANES, LANES)
        if stage == 0:
            field, row = j // (2 * groups), 3 * ((j // groups) % 2)
        elif stage == 1:
            field, row = 2, j // groups
        else:
            field, row = j // (2 * groups), 1 + (j // groups) % 2
        return field, row * 8, column

    def partner(i):
        planes = n // 4
        turn = i // 4
        away = (turn + 1) // 2
        ahead = jnp.where(turn % 2 == 1, away, planes - away)
        z = (dom // 4 + ahead) % planes
        return z * 4 + (dom % 4 + i % 4) % 4

    barrier = pltpu.get_barrier_semaphore()

    for i in range(n - 1, 0, -1):
        pl.semaphore_signal(barrier, 1, device_id={"dom": partner(i)})
    for i in range(1, tiles):
        pl.semaphore_signal(barrier, 1, device_id={"tile": (tile + i) % tiles})

    noise_copy = pltpu.make_async_copy(noise, noise_all.at[:, HALO:HALO + 32, :], local_sem.at[0])
    small_copies = [
        pltpu.make_async_copy(source, there, local_sem.at[1 + at])
        for at, (source, there) in enumerate(
            ((parents_in, parents), (position_in, position), (value_in, value), (precision_in, precision))
        )
    ]
    for copy in small_copies:
        copy.start()
    noise_copy.start()
    pl.semaphore_wait(barrier, n - 1 + tiles - 1)

    def spread(stage):
        def piece(j):
            field, row, column = place(stage, j)
            return state.at[:, field, pl.ds(pl.multiple_of(row, 8), 8), pl.ds(column, LANES)]

        mine = every[stage].at[pl.ds(2 * dom, 2)]

        @pl.loop(1, n)
        def _(i):
            target = partner(i)
            pltpu.make_async_remote_copy(
                piece(target), mine, spread_send.at[stage], spread_recv.at[stage], device_id={"dom": target}
            ).start()

        pltpu.make_async_copy(piece(dom), mine, spread_recv.at[stage]).start()

    def give_back(stage, first, count, sem):
        field, row, column = place(stage, dom)
        rows, lanes = pl.ds(pl.multiple_of(row, 8), 8), pl.ds(column, LANES)
        rows = pl.ds(pl.multiple_of(HALO + row, 8), 8)
        there = fields.at[pl.ds(first, count), field, rows, lanes]

        @pl.loop(0, n)
        def _(i):
            target = (i // 4) * 4 + (dom + i) % 4

            @pl.when(target != dom)
            def _():
                pltpu.make_async_remote_copy(
                    pick[stage].at[pl.ds(2 * target + first, count)], there,
                    back_send.at[sem], back_recv.at[sem], device_id={"dom": target},
                ).start()

        pltpu.make_async_copy(pick[stage].at[pl.ds(2 * dom + first, count)], there, back_recv.at[sem]).start()

    def choose(stage):
        pltpu.make_async_copy(every[stage], every[stage], spread_recv.at[stage]).wait()

        @pl.loop(0, 2 * n, unroll=8)
        def _(s):
            pick[stage][s] = every[stage][parents[s]]

    def await_back(sem, count):
        whole = pick[0].at[pl.ds(0, count * n)]
        pltpu.make_async_copy(whole, whole, back_recv.at[sem]).wait()

    def to_above(kind, source, there):
        return pltpu.make_async_remote_copy(
            source, there, halo_send.at[kind, 0], halo_recv.at[kind, 0], device_id={"tile": jnp.maximum(tile - 1, 0)}
        )

    def to_below(kind, source, there):
        return pltpu.make_async_remote_copy(
            source, there, halo_send.at[kind, 1], halo_recv.at[kind, 1],
            device_id={"tile": jnp.minimum(tile + 1, tiles - 1)},
        )

    top, bottom = pl.ds(HALO, HALO), pl.ds(HALO + 24, HALO)
    over, under = pl.ds(0, HALO), pl.ds(HALO + 32, HALO)

    def halos(kind):
        if kind == NOISE:
            up = to_above(kind, noise.at[:, pl.ds(0, HALO), :], noise_all.at[:, under, :])
            down = to_below(kind, noise.at[:, pl.ds(24, HALO), :], noise_all.at[:, over, :])
        elif kind == GAIN:
            up = to_above(kind, nudge.at[:, top, :], nudge.at[:, under, :])
            down = to_below(kind, nudge.at[:, bottom, :], nudge.at[:, over, :])
        else:
            which = pl.ds(0, 2) if kind == FIRST else pl.ds(2, 1)
            up = to_above(kind, fields.at[:, which, top, :], fields.at[:, which, under, :])
            down = to_below(kind, fields.at[:, which, bottom, :], fields.at[:, which, over, :])
        return up, down

    def send_halo(kind):
        up, down = halos(kind)

        @pl.when(has_above)
        def _():
            up.start()

        @pl.when(has_below)
        def _():
            down.start()

    def await_halo(kind):
        up, down = halos(kind)

        @pl.when(has_below)
        def _():
            up.wait_recv()

        @pl.when(has_above)
        def _():
            down.wait_recv()

    def await_halo_sent(kind):
        up, down = halos(kind)

        @pl.when(has_above)
        def _():
            up.wait_send()

        @pl.when(has_below)
        def _():
            down.wait_send()

    spread(0)
    spread(1)
    send_halo(NOISE)

    @pl.when(tile == 0)
    def _():
        fields[:, :, 0:HALO, :] = jnp.zeros((2, 3, HALO, cols), jnp.float32)
        noise_all[:, 0:HALO, :] = jnp.zeros((2, HALO, cols), jnp.float32)
        nudge[:, 0:HALO, :] = jnp.zeros((2, HALO, cols), jnp.float32)

    @pl.when(tile == tiles - 1)
    def _():
        fields[:, :, HALO + 32:, :] = jnp.zeros((2, 3, HALO, cols), jnp.float32)
        noise_all[:, HALO + 32:, :] = jnp.zeros((2, HALO, cols), jnp.float32)
        nudge[:, HALO + 32:, :] = jnp.zeros((2, HALO, cols), jnp.float32)

    for copy in small_copies:
        copy.wait()

    local = position[...] - tile * (32 * cols)
    row_of = local // cols
    column_of = local % cols
    in_row = lax.broadcasted_iota(jnp.int32, (32, obs), 0) == row_of

    def put(slot, row):
        spread_row = jnp.where(in_row, row.astype(jnp.float32), 0.0)
        row_values[slot * 32:(slot + 1) * 32, :] = spread_row.astype(jnp.bfloat16)

    put(0, jnp.ones((1, obs), jnp.float32))
    for at, part in enumerate(split_three(value[...])):
        put(1 + at, part)
    for at, part in enumerate(split_three(precision[...])):
        put(4 + at, part)

    wide = min(cols, 256)

    @pl.loop(0, cols // wide)
    def _(block):
        first = pl.multiple_of(block * wide, wide)
        column = lax.broadcasted_iota(jnp.int32, (wide, obs), 0) + first
        in_column = jnp.where(column == column_of, 1.0, 0.0).astype(jnp.bfloat16)
        grid = lax.dot_general(
            row_values[...], in_column, (((1,), (1,)), ((), ())), preferred_element_type=jnp.float32
        )
        lanes = pl.ds(first, wide)
        nudge[0, HALO:HALO + 32, lanes] = RELAXATION * grid[0:32]
        nudge[1, HALO:HALO + 32, lanes] = (grid[32:64] + grid[64:96]) + grid[96:128]
        weight[:, lanes] = (grid[128:160] + grid[160:192]) + grid[192:224]

    send_halo(GAIN)

    choose(0)
    give_back(0, 0, 2, 0)
    spread(2)
    choose(1)
    give_back(1, 0, 2, 1)
    await_back(0, 2)
    send_halo(FIRST)
    choose(2)
    give_back(2, 0, 1, 2)
    give_back(2, 1, 1, 3)
    await_back(1, 2)
    send_halo(SECOND)

    noise_copy.wait()
    for kind in range(4):
        await_halo(kind)

    row_id = lax.broadcasted_iota(jnp.int32, (TALL, cols), 0)
    inside = jnp.logical_and(
        jnp.logical_or(row_id >= HALO, has_above), jnp.logical_or(row_id < HALO + 32, has_below)
    )

    def column_change(a):
        return pltpu.roll(a, cols - 1, 1) - pltpu.roll(a, 1, 1)

    def row_change(a):
        return pltpu.roll(a, TALL - 1, 0) - pltpu.roll(a, 1, 0)

    half = 0.5 * COURANT

    def sums_copy(p, i):
        mine = sums.at[p, tile]
        return pltpu.make_async_remote_copy(
            mine, mine, sums_send.at[p], sums_recv.at[p], device_id={"tile": (tile + i) % tiles}
        )

    def forecast(p):
        for step in range(STEPS):
            if step == 0:
                h, u, v = fields[p, 0] + noise_all[p], fields[p, 1], fields[p, 2]
            else:
                h, u, v = work[0], work[1], work[2]
            h1 = h - half * (column_change(u) + row_change(v))
            h2 = h1 + nudge[0] * (nudge[1] - h1)
            if step == STEPS - 1:
                h2 = h2[HALO:HALO + 32]
                miss = nudge[1, HALO:HALO + 32, :] - h2
                miss = weight[...] * (miss * miss)
                total = jnp.zeros((8, LANES), jnp.float32)
                for r in range(4):
                    for c in range(groups):
                        total = total + miss[8 * r:8 * r + 8, LANES * c:LANES * (c + 1)]
                sums[p, tile] = total
                for i in sorted(range(1, tiles), key=lambda i: -min(i, tiles - i)):
                    sums_copy(p, i).start()
            u1 = u + CORIOLIS * v - half * column_change(h1)
            v1 = v - CORIOLIS * u - half * row_change(h1)
            if step < STEPS - 1:
                work[0] = jnp.where(inside, h2, 0.0)
                work[1] = jnp.where(inside, u1, 0.0)
                work[2] = jnp.where(inside, v1, 0.0)
            else:
                result[p, 0] = h2
                result[p, 1] = u1[HALO:HALO + 32]
                result[p, 2] = v1[HALO:HALO + 32]

    await_back(2, 1)
    forecast(0)
    await_back(3, 1)
    forecast(1)

    for p in range(2):
        others = sums.at[p, pl.ds(0, tiles - 1)]
        pltpu.make_async_copy(others, others, sums_recv.at[p]).wait()
        total = sums[p, 0]
        for t in range(1, tiles):
            total = total + sums[p, t]
        mismatch_out[p] = total * (0.5 / obs_all)

    for p in range(2):
        others = sums.at[p, pl.ds(0, tiles - 1)]
        pltpu.make_async_copy(others, others, sums_send.at[p]).wait()
    two = pick[0].at[pl.ds(0, 2 * (n - 1))]
    one = pick[0].at[pl.ds(0, n - 1)]
    for stage in range(3):
        pltpu.make_async_copy(two, two, spread_send.at[stage]).wait()
    for sem in range(4):
        sent = two if sem < 2 else one
        pltpu.make_async_copy(sent, sent, back_send.at[sem]).wait()
    for kind in range(4):
        await_halo_sent(kind)


def body(state, noise, parents, measured_cell_position, obs_value, obs_precision):
    n, tiles = lax.axis_size("dom"), lax.axis_size("tile")
    cols = state.shape[3]
    obs = measured_cell_position.shape[0]
    f32 = jnp.float32
    vmem = pl.BlockSpec(memory_space=pltpu.VMEM)
    hbm = pl.BlockSpec(memory_space=pltpu.HBM)
    dma = pltpu.SemaphoreType.DMA
    pieces = pltpu.VMEM((2 * n, 8, LANES), f32)
    fields, sums = pl.pallas_call(
        functools.partial(kernel, n, tiles, cols, obs, obs * tiles),
        out_shape=(
            pltpu.VMEM(state.shape, f32),
            pltpu.VMEM((2, 8, LANES), f32),
        ),
        in_specs=[hbm] * 6,
        out_specs=(vmem, vmem),
        scratch_shapes=[
            pltpu.SMEM((2 * n,), jnp.int32),
            pltpu.VMEM((1, obs), jnp.int32),
            pltpu.VMEM((1, obs), f32),
            pltpu.VMEM((1, obs), f32),
            pieces, pieces, pieces, pieces, pieces, pieces,
            pltpu.VMEM((2, 3, TALL, cols), f32),
            pltpu.VMEM((2, TALL, cols), f32),
            pltpu.VMEM((2, TALL, cols), f32),
            pltpu.VMEM((32, cols), f32),
            pltpu.VMEM((7 * 32, obs), jnp.bfloat16),
            pltpu.VMEM((3, TALL, cols), f32),
            pltpu.VMEM((2, tiles, 8, LANES), f32),
            dma((3,)), dma((3,)), dma((5,)), dma((4,)), dma((4,)),
            dma((4, 2)), dma((4, 2)), dma((2,)), dma((2,)),
        ],
        compiler_params=pltpu.CompilerParams(
            collective_id=0, has_side_effects=True, vmem_limit_bytes=32 * 1024 * 1024
        ),
    )(*(
        pltpu.with_memory_space_constraint(operand, pltpu.HBM)
        for operand in (
            parents,
            measured_cell_position.reshape(1, obs),
            obs_value.reshape(1, obs),
            obs_precision.reshape(1, obs),
            state,
            noise,
        )
    ))
    return fields, jnp.sum(sums, axis=(1, 2))


def solution(mesh):
    placed = (
        P("dom", None, "tile", None),
        P("dom", "tile", None),
        P(),
        P("tile"),
        P("tile"),
        P("tile"),
    )
    return jax.shard_map(
        body,
        mesh=mesh,
        in_specs=placed,
        out_specs=(P("dom", None, "tile", None), P("dom")),
        check_vma=False,
    )
```

profile of v0, /device:TPU:1, one launch (start us, length us, event | category | flops | bytes accessed | tf_op | source)
XLA Modules:
  0.0 55.5 jit_solution(4349384406506532970)
XLA Ops:
  0.6 53.3 %shard_map.77 = (f32[2,3,32,1024]{3,2,1,0:T(8,128)S(1)}, f32[2,8,128]{2,1,0:T(8,128)S(1)}) custom-call(s32[64]{0:T(128)} %parents_in.1, s32[1,2048]{1,0:T(1,128)} %bitcast.3, f32[1,2048]{1,0:T(1,128)} %bitcast.4, f32[1,2048]{1,0:T(1,128)} %bitcast.5, f32[2,3,32,1024]{3,2,1,0:T(8,128)} %state.1, f32[2,32,1024]{2,1,0:T(8,128)} %noise.1), custom_call_target="tpu_custom_call" | custom-call | tf_op jit(solution)/shard_map/pallas_call | solution.py:342
  54.0 0.9 %copy.9 = f32[2,3,32,1024]{3,2,1,0:T(8,128)} copy(f32[2,3,32,1024]{3,2,1,0:T(8,128)S(1)} %get-tuple-element.6) | data formatting | bytes 1572864
  54.9 0.6 %reduce_sum.9 = f32[2]{0:T(128)} reduce(f32[2,8,128]{2,1,0:T(8,128)S(1)} %get-tuple-element.5, f32[]{:T(128)} %constant.0.clone.1), dimensions={1,2}, to_apply=%region_0.0 | reduce | flops 2046 | bytes 8204 | tf_op jit(solution)/shard_map/reduce_sum | solution.py:380
where the time goes:
time: 55.5 us
  Pallas kernels  53.3 us (96%)
  local copies, waits for them, and re-layouts  0.88 us (2%)
  between operations  0.64 us (1%)
  other arithmetic  0.61 us (1%)
    pallas_call x1, Pallas kernels, body(): pl.pallas_call(functools.partial(kernel, n, tiles, cols, obs, obs * tiles...  53.3 us

commit v1 on v0

--- a/solution.py
+++ b/solution.py
@@ -328,6 +328,20 @@
         pltpu.make_async_copy(sent, sent, back_send.at[sem]).wait()
     for kind in range(4):
         await_halo_sent(kind)
+
+
+def finish(fields, sums, fields_out, mismatch_out, both, sem):
+    copies = [
+        pltpu.make_async_copy(fields.at[p, f], fields_out.at[p, f], sem.at[3 * p + f]) for p in range(2) for f in range(3)
+    ]
+    for copy in copies:
+        copy.start()
+    for p in range(2):
+        both[p] = jnp.sum(sums[p])
+    copies.append(pltpu.make_async_copy(both, mismatch_out, sem.at[6]))
+    copies[-1].start()
+    for copy in copies:
+        copy.wait()
 
 
 def body(state, noise, parents, measured_cell_position, obs_value, obs_precision):
@@ -377,7 +391,13 @@
             noise,
         )
     ))
-    return fields, jnp.sum(sums, axis=(1, 2))
+    return pl.pallas_call(
+        finish,
+        out_shape=(jax.ShapeDtypeStruct(state.shape, f32), jax.ShapeDtypeStruct((2,), f32)),
+        in_specs=[vmem, vmem],
+        out_specs=(hbm, hbm),
+        scratch_shapes=[pltpu.SMEM((2,), f32), dma((7,))],
+    )(pltpu.with_memory_space_constraint(fields, pltpu.VMEM), pltpu.with_memory_space_constraint(sums, pltpu.VMEM))
 
 
 def solution(mesh):

time: 55.5 us -> 55 us (level)
  Pallas kernels: 53.3 us -> 54.3 us
  local copies, waits for them, and re-layouts: 0.88 us -> 0 us
  other arithmetic: 0.61 us -> 0 us
    pallas_call x0 -> x1, Pallas kernels: none -> 0.94 us  [body(): pl.pallas_call(finish, out_shape=(jax.ShapeDtypeStruct(state.shape, f32),...]
    unnamed x1 -> x0, local copies, waits for them, and re-layouts: 0.88 us -> none
    reduce_sum x1 -> x0, other arithmetic: 0.61 us -> none  [body(): return (fields, jnp.sum(sums, axis=(1, 2)))]
where the time goes in v1:
time: 55 us; the launch traced here: 54.9 us
  Pallas kernels  54.3 us (99%)
  between operations  0.64 us (1%)
    pallas_call x1, Pallas kernels, body(): pl.pallas_call(functools.partial(kernel, n, tiles, cols, obs, obs * tiles...  53.3 us

profile of v1, /device:TPU:1, one launch (start us, length us, event | category | flops | bytes accessed | tf_op | source)
XLA Modules:
  0.0 54.9 jit_solution(16298313340667586903)
XLA Ops:
  0.6 53.3 %shard_map.77 = (f32[2,3,32,1024]{3,2,1,0:T(8,128)S(1)}, f32[2,8,128]{2,1,0:T(8,128)S(1)}) custom-call(s32[64]{0:T(128)} %parents_in.1, s32[1,2048]{1,0:T(1,128)} %bitcast.3, f32[1,2048]{1,0:T(1,128)} %bitcast.4, f32[1,2048]{1,0:T(1,128)} %bitcast.5, f32[2,3,32,1024]{3,2,1,0:T(8,128)} %state.1, f32[2,32,1024]{2,1,0:T(8,128)} %noise.1), custom_call_target="tpu_custom_call" | custom-call | tf_op jit(solution)/shard_map/pallas_call | solution.py:356
  54.0 0.9 %shard_map.78 = (f32[2,3,32,1024]{3,2,1,0:T(8,128)}, f32[2]{0:T(128)}) custom-call(f32[2,3,32,1024]{3,2,1,0:T(8,128)S(1)} %get-tuple-element.4.fields, f32[2,8,128]{2,1,0:T(8,128)S(1)} %get-tuple-element.5.sums), custom_call_target="tpu_custom_call" | custom-call | tf_op jit(solution)/shard_map/pallas_call | solution.py:394

commit v2 on v1

--- a/solution.py
+++ b/solution.py
@@ -87,24 +87,34 @@
 
         mine = every[stage].at[pl.ds(2 * dom, 2)]
 
-        @pl.loop(1, n)
-        def _(i):
-            target = partner(i)
-            pltpu.make_async_remote_copy(
-                piece(target), mine, spread_send.at[stage], spread_recv.at[stage], device_id={"dom": target}
-            ).start()
-
-        pltpu.make_async_copy(piece(dom), mine, spread_recv.at[stage]).start()
-
-    def give_back(stage, first, count, sem):
-        field, row, column = place(stage, dom)
-        rows, lanes = pl.ds(pl.multiple_of(row, 8), 8), pl.ds(column, LANES)
-        rows = pl.ds(pl.multiple_of(HALO + row, 8), 8)
-        there = fields.at[pl.ds(first, count), field, rows, lanes]
-
         @pl.loop(0, n)
         def _(i):
             target = (i // 4) * 4 + (dom + i) % 4
+
+            @pl.when(target != dom)
+            def _():
+                pltpu.make_async_remote_copy(
+                    piece(target), mine, spread_send.at[stage], spread_recv.at[stage], device_id={"dom": target}
+                ).start()
+
+        pltpu.make_async_copy(piece(dom), mine, spread_recv.at[stage]).start()
+
+    def await_spread(stage):
+        pltpu.make_async_copy(every[stage], every[stage], spread_recv.at[stage]).wait()
+
+    def give_back(stage, first, count, sem):
+        field, row, column = place(stage, dom)
+        rows, lanes = pl.ds(pl.multiple_of(HALO + row, 8), 8), pl.ds(column, LANES)
+        there = fields.at[pl.ds(first, count), field, rows, lanes]
+
+        def choose(target):
+            for p in range(first, first + count):
+                pick[stage][2 * target + p] = every[stage][parents[2 * target + p]]
+
+        @pl.loop(0, n)
+        def _(i):
+            target = (i // 4) * 4 + (dom + i) % 4
+            choose(target)
 
             @pl.when(target != dom)
             def _():
@@ -114,13 +124,6 @@
                 ).start()
 
         pltpu.make_async_copy(pick[stage].at[pl.ds(2 * dom + first, count)], there, back_recv.at[sem]).start()
-
-    def choose(stage):
-        pltpu.make_async_copy(every[stage], every[stage], spread_recv.at[stage]).wait()
-
-        @pl.loop(0, 2 * n, unroll=8)
-        def _(s):
-            pick[stage][s] = every[stage][parents[s]]
 
     def await_back(sem, count):
         whole = pick[0].at[pl.ds(0, count * n)]
@@ -237,14 +240,14 @@
 
     send_halo(GAIN)
 
-    choose(0)
+    await_spread(0)
     give_back(0, 0, 2, 0)
     spread(2)
-    choose(1)
+    await_spread(1)
     give_back(1, 0, 2, 1)
     await_back(0, 2)
     send_halo(FIRST)
-    choose(2)
+    await_spread(2)
     give_back(2, 0, 1, 2)
     give_back(2, 1, 1, 3)
     await_back(1, 2)

time: 55 us -> 54.6 us (level)
  no operation moved by 1% of the time
where the time goes in v2:
time: 54.6 us; the launch traced here: 54.5 us
  Pallas kernels  53.9 us (99%)
  between operations  0.64 us (1%)
    pallas_call x1, Pallas kernels, body(): pl.pallas_call(functools.partial(kernel, n, tiles, cols, obs, obs * tiles...  53 us

profile of v2, /device:TPU:1, one launch (start us, length us, event | category | flops | bytes accessed | tf_op | source)
XLA Modules:
  0.0 54.5 jit_solution(13673100903673310456)
XLA Ops:
  0.6 53.0 %shard_map.77 = (f32[2,3,32,1024]{3,2,1,0:T(8,128)S(1)}, f32[2,8,128]{2,1,0:T(8,128)S(1)}) custom-call(s32[64]{0:T(128)} %parents_in.1, s32[1,2048]{1,0:T(1,128)} %bitcast.3, f32[1,2048]{1,0:T(1,128)} %bitcast.4, f32[1,2048]{1,0:T(1,128)} %bitcast.5, f32[2,3,32,1024]{3,2,1,0:T(8,128)} %state.1, f32[2,32,1024]{2,1,0:T(8,128)} %noise.1), custom_call_target="tpu_custom_call" | custom-call | tf_op jit(solution)/shard_map/pallas_call | solution.py:359
  53.6 0.9 %shard_map.78 = (f32[2,3,32,1024]{3,2,1,0:T(8,128)}, f32[2]{0:T(128)}) custom-call(f32[2,3,32,1024]{3,2,1,0:T(8,128)S(1)} %get-tuple-element.4.fields, f32[2,8,128]{2,1,0:T(8,128)S(1)} %get-tuple-element.5.sums), custom_call_target="tpu_custom_call" | custom-call | tf_op jit(solution)/shard_map/pallas_call | solution.py:397

commit v3 on v2

--- a/solution.py
+++ b/solution.py
@@ -249,9 +249,9 @@
     send_halo(FIRST)
     await_spread(2)
     give_back(2, 0, 1, 2)
-    give_back(2, 1, 1, 3)
     await_back(1, 2)
     send_halo(SECOND)
+    give_back(2, 1, 1, 3)
 
     noise_copy.wait()
     for kind in range(4):

time: 54.6 us -> 57.2 us (1.048)
  Pallas kernels: 53.9 us -> 56.5 us
    pallas_call x1, Pallas kernels: 53 us -> 55.6 us  [body(): pl.pallas_call(functools.partial(kernel, n, tiles, cols, obs, obs * tiles...]
where the time goes in v3:
time: 57.2 us; the launch traced here: 57.1 us
  Pallas kernels  56.5 us (99%)
  between operations  0.64 us (1%)
    pallas_call x1, Pallas kernels, body(): pl.pallas_call(functools.partial(kernel, n, tiles, cols, obs, obs * tiles...  55.6 us

profile of v3, /device:TPU:1, one launch (start us, length us, event | category | flops | bytes accessed | tf_op | source)
XLA Modules:
  0.0 57.1 jit_solution(14896825938822550681)
XLA Ops:
  0.6 55.6 %shard_map.77 = (f32[2,3,32,1024]{3,2,1,0:T(8,128)S(1)}, f32[2,8,128]{2,1,0:T(8,128)S(1)}) custom-call(s32[64]{0:T(128)} %parents_in.1, s32[1,2048]{1,0:T(1,128)} %bitcast.3, f32[1,2048]{1,0:T(1,128)} %bitcast.4, f32[1,2048]{1,0:T(1,128)} %bitcast.5, f32[2,3,32,1024]{3,2,1,0:T(8,128)} %state.1, f32[2,32,1024]{2,1,0:T(8,128)} %noise.1), custom_call_target="tpu_custom_call" | custom-call | tf_op jit(solution)/shard_map/pallas_call | solution.py:359
  56.2 0.9 %shard_map.78 = (f32[2,3,32,1024]{3,2,1,0:T(8,128)}, f32[2]{0:T(128)}) custom-call(f32[2,3,32,1024]{3,2,1,0:T(8,128)S(1)} %get-tuple-element.4.fields, f32[2,8,128]{2,1,0:T(8,128)S(1)} %get-tuple-element.5.sums), custom_call_target="tpu_custom_call" | custom-call | tf_op jit(solution)/shard_map/pallas_call | solution.py:397
